TPU v7x, 32 devices: a whole 2x2x4 slice. The times are simulated.
32 devices in a mesh: aux: 4 (over y, x), row: 8 (over z, core).
Axes of the slice: x: 2, y: 2, z: 4, core: 2. Of those that a mesh axis runs over, the one named last changes fastest.
Arguments:
- b_tiles: bfloat16 [4, 8192, 2048], P('aux', 'row'), may hold values from -0.125 to 0.125
- occ_coeff: bfloat16 [8192, 256], P('row'), may hold values from -3 to 3
- tile_blocks: int32 [64, 16], P('row'), may hold values from 0 to 63, as said below
- screen_mask: int32 [64, 16], P('row'), may hold values from 0 to 1, as said below
Outputs:
- exchange: bfloat16 [8192, 8, 4, 256], P('row', None, 'aux')
Inputs may be any that keep to these rules, and one draw needn't show every extreme that they name: `tile_blocks`: each entry names a basis block at most 8 blocks away from its own row's block; the first slot of every block names the block itself. `screen_mask`: in every basis block the kept slots come first; some block keeps all 16.
All inputs are finite; a program needn't handle non-finite values.
Results may differ from a plain program's by a relative error of at most 0.0057.
Values may be sent and summed in bfloat16 or wider, within the bound.
A program may use at most 128 MiB of HBM per device.

v0:
```python
import jax
import jax.numpy as jnp
from jax import lax
from jax.sharding import PartitionSpec as P


def with_halo(block, sides, width):
    for axis, dim in sides:
        count = lax.axis_size(axis)
        forward = [(i, i + 1) for i in range(count - 1)]
        backward = [(target, source) for source, target in forward]
        low = lax.ppermute(
            lax.slice_in_dim(block, block.shape[dim] - width, None, axis=dim), axis, forward
        )
        high = lax.ppermute(lax.slice_in_dim(block, 0, width, axis=dim), axis, backward)
        block = jnp.concatenate([low, block, high], axis=dim)
    return block


def per_device(b_tiles, occ_coeff, tile_blocks, screen_mask):
    p_local, rows_local, stored = b_tiles.shape
    blocks_local, slot_count = tile_blocks.shape
    block_size = rows_local // blocks_local
    orbitals = occ_coeff.shape[1]
    row_count = lax.axis_size("row")
    aux_count = lax.axis_size("aux")
    extended = with_halo(occ_coeff, (("row", 0),), rows_local)
    coeff_blocks = extended.reshape(3 * blocks_local, block_size, orbitals)
    local_index = tile_blocks - (lax.axis_index("row") - 1) * blocks_local
    picked = jnp.take(coeff_blocks, local_index, axis=0)
    keep_mask = screen_mask.astype(jnp.bfloat16)
    tiles_five = b_tiles.reshape(p_local, blocks_local, block_size, slot_count, block_size)
    masked = picked * keep_mask[:, :, None, None]
    half_sum = jnp.einsum(
        "pbmsn,bsni->pbmi", tiles_five, masked, preferred_element_type=jnp.float32
    )
    half_local = half_sum.astype(jnp.bfloat16).reshape(p_local, rows_local, orbitals)
    slab_rows = lax.all_gather(half_local, "aux", axis=0, tiled=True)
    share = rows_local // aux_count
    all_rows = lax.all_gather(half_local, "row", axis=1, tiled=True)
    split_rows = all_rows.reshape(p_local, row_count, aux_count, share, orbitals)
    regrouped = lax.all_to_all(split_rows, "aux", split_axis=2, concat_axis=0, tiled=True)
    partner = regrouped.reshape(p_local * aux_count, row_count * share, orbitals)
    result = jnp.einsum("pmi,pli->ml", slab_rows, partner, preferred_element_type=jnp.float32)
    return result.astype(jnp.bfloat16).reshape(rows_local, row_count, 1, share)


def solution(mesh):
    in_specs = (P("aux", "row", None), P("row", None), P("row", None), P("row", None))
    out_specs = P("row", None, "aux", None)
    return jax.shard_map(
        per_device, mesh=mesh, in_specs=in_specs, out_specs=out_specs, check_vma=False
    )
```

profile of v0, /device:TPU:0, one launch (start us, length us, event | category | flops | bytes accessed | tf_op | source)
XLA Modules:
  0.0 175.2 jit_solution(3235418467693490283)
XLA Ops:
  6.5 0.0 all-gather.5.cloned.1.call-start
  6.5 2.4 %collective-permute-start = (bf16[1024,256]{1,0:T(8,128)(2,1)}, bf16[1024,256]{1,0:T(8,128)(2,1)S(1)}, u32[]{:S(2)}, u32[]{:S(2)}) collective-permute-start(bf16[1024,256]{1,0:T(8,128)(2,1)} %param.5), channel_id=1, source_target_pairs={{0,1},{1,2},{2,3},{3,4},{4,5},{5,6},{6,7},{8,9},{9,10},{10,11},{11... | collective-permute-start | bytes 1572872 | tf_op jit(solution)/shard_map/ppermute | solution.py:12
  8.9 1.3 collective-permute-start.1
  10.2 0.7 compare_and_fusion
  10.9 0.1 reshape.37
  11.0 0.0 copy-start.1
  11.0 5.7 %copy.12 = bf16[128,8,16,128]{3,2,1,0:T(8,128)(2,1)} copy(bf16[128,8,16,128]{3,1,2,0:T(8,128)(2,1)} %bitcast.34) | data formatting | bytes 8388608
  16.7 0.0 copy-done.1
  16.7 0.0 collective-permute-done
  16.7 0.0 collective-permute-done.1
  16.7 0.0 copy-done
  16.7 0.1 pad_maximum_fusion
  16.8 6.5 %gather_fusion = bf16[128,128,256]{2,1,0:T(8,128)(2,1)} fusion(bf16[24,128,256]{2,1,0:T(8,128)(2,1)S(1)} %bitcast.32, s32[1024]{0:T(1024)S(1)} %pad_clamp_fusion), kind=kCustom, calls=%fused_computation | custom fusion | bytes 16777728 | tf_op jit(solution)/shard_map/jit(_take)/gather | solution.py:30
  23.4 8.2 %fusion.12 = bf16[8,256,128]{1,2,0:T(8,128)(2,1)} fusion(bf16[8,16,128,256]{3,2,1,0:T(8,128)(2,1)} %bitcast.33, pred[8,16]{1,0:T(8,128)(4,1)S(1)} %get-tuple-element.5, bf16[8,16]{1,0:T(8,128)(2,1)S(1)} %convert_element_type.15, bf16[8,128,16,128]{3,2,1,0:T(8,128)(2,1)} %bitcast.35), kind=kOutput, calls=%fused_computation.11 | convolution fusion | flops 1094975488 | bytes 13107584 | tf_op jit(solution)/shard_map/pbmsn,bsni->pbmi/dot_general | solution.py:34
  31.6 0.0 all-gather.5.cloned.1.call-update
  31.6 0.0 all-gather.3.cloned.1.call-start
  31.6 0.7 all-gather.3.cloned.1.call-update
  32.3 52.0 %all-gather.5.cloned.1.call-done = bf16[1,8192,256]{2,1,0:T(8,128)(2,1)} async-done(((bf16[1,1024,256]{2,1,0:T(8,128)(2,1)}), bf16[1,8192,256]{2,1,0:T(8,128)(2,1)}) %all-gather.5.cloned.1.call-update) | async-done | bytes 4194320 | tf_op jit(solution)/shard_map/all_gather | solution.py:40
  84.3 4.6 %copy.9 = bf16[1,8,4,256,256]{4,3,1,0,2:T(8,128)(2,1)} copy(bf16[1,8,4,256,256]{4,3,2,1,0:T(8,128)(2,1)} %bitcast.36) | data formatting | bytes 8388608 | tf_op jit(solution)/shard_map/reshape | solution.py:41
  89.0 4.9 %all-to-all-start = ((bf16[1,8,4,256,256]{4,3,1,0,2:T(8,128)(2,1)}), bf16[1,8,4,256,256]{4,3,1,0,2:T(8,128)(2,1)}, u32[]{:S(2)}, u32[]{:S(2)}) async-start(bf16[1,8,4,256,256]{4,3,1,0,2:T(8,128)(2,1)} %copy.9), calls=%async_computation | async-start | bytes 8388608 | tf_op jit(solution)/shard_map/all_to_all | solution.py:42
  93.9 63.7 %all-gather.3.cloned.1.call-done = bf16[4,1024,256]{2,1,0:T(8,128)(2,1)} async-done(((bf16[1,1024,256]{2,1,0:T(8,128)(2,1)}), bf16[4,1024,256]{2,1,0:T(8,128)(2,1)}) %all-gather.3.cloned.1.call-update) | async-done | bytes 2097168 | tf_op jit(solution)/shard_map/all_gather | solution.py:38
  157.6 0.0 all-to-all-done
  157.6 7.3 %bitcast_convert_fusion = bf16[1024,2048]{1,0:T(8,128)(2,1)S(1)} fusion(bf16[4,1024,256]{2,1,0:T(8,128)(2,1)} %all-gather.3.cloned.1.call-done, bf16[4,2048,256]{2,1,0:T(8,128)(2,1)} %bitcast.12), kind=kOutput, calls=%fused_computation.1 | convolution fusion | flops 4297064448 | bytes 10485760 | tf_op jit(solution)/shard_map/pmi,pli->ml/dot_general | solution.py:44
  164.9 3.5 %copy.13 = bf16[128,8,8,256]{3,2,1,0:T(8,128)(2,1)} copy(bf16[128,8,8,256]{3,1,2,0:T(8,128)(2,1)S(1)} %bitcast.37) | data formatting | bytes 8388608
  (3 shorter events, 0.0 us)
Async XLA Ops:
  6.5 77.8 %all-gather.5.cloned.1.call-start = ((), (), s32[]{:S(2)}) async-start(), calls=%async_computation.2 | async-start | bytes 4718592 | tf_op jit(solution)/shard_map/all_gather | solution.py:40
  6.5 10.2 %collective-permute-start = (bf16[1024,256]{1,0:T(8,128)(2,1)}, bf16[1024,256]{1,0:T(8,128)(2,1)S(1)}, u32[]{:S(2)}, u32[]{:S(2)}) collective-permute-start(bf16[1024,256]{1,0:T(8,128)(2,1)} %param.5), channel_id=1, source_target_pairs={{0,1},{1,2},{2,3},{3,4},{4,5},{5,6},{6,7},{8,9},{9,10},{10,11},{11... | collective-permute-start | bytes 1572872 | tf_op jit(solution)/shard_map/ppermute | solution.py:12
  8.9 7.8 %collective-permute-start.1 = (bf16[1024,256]{1,0:T(8,128)(2,1)}, bf16[1024,256]{1,0:T(8,128)(2,1)S(1)}, u32[]{:S(2)}, u32[]{:S(2)}) collective-permute-start(bf16[1024,256]{1,0:T(8,128)(2,1)} %param.5), channel_id=1, source_target_pairs={{1,0},{2,1},{3,2},{4,3},{5,4},{6,5},{7,6},{9,8},{10,9},{11,10},{12... | collective-permute-start | bytes 1572872 | tf_op jit(solution)/shard_map/ppermute | solution.py:15
  11.0 5.7 %copy-start.1 = (s32[8,16]{1,0:T(8,128)S(1)}, s32[8,16]{1,0:T(8,128)}, u32[]{:S(2)}) copy-start(s32[8,16]{1,0:T(8,128)} %param.7) | copy-start | bytes 1540
  11.0 5.7 %copy-start = (bf16[1024,256]{1,0:T(8,128)(2,1)S(1)}, bf16[1024,256]{1,0:T(8,128)(2,1)}, u32[]{:S(2)}) copy-start(bf16[1024,256]{1,0:T(8,128)(2,1)} %param.5) | copy-start | bytes 1572868
  31.6 126.0 %all-gather.3.cloned.1.call-start = ((), (), s32[]{:S(2)}) async-start(), calls=%async_computation.1 | async-start | bytes 2621440 | tf_op jit(solution)/shard_map/all_gather | solution.py:38
  89.0 68.6 %all-to-all-start = ((bf16[1,8,4,256,256]{4,3,1,0,2:T(8,128)(2,1)}), bf16[1,8,4,256,256]{4,3,1,0,2:T(8,128)(2,1)}, u32[]{:S(2)}, u32[]{:S(2)}) async-start(bf16[1,8,4,256,256]{4,3,1,0,2:T(8,128)(2,1)} %copy.9), calls=%async_computation | async-start | bytes 8388608 | tf_op jit(solution)/shard_map/all_to_all | solution.py:42
Sparse Core Ops, SparseCore 0:
  31.7 52.5 all-gather.4
  86.2 71.3 all-gather.2
where the time goes:
time: 176 us; the launch traced here: 175 us
  waiting for transfers between devices  116 us (66%)
  local copies, waits for them, and re-layouts  20.4 us (12%)
  matrix products  15.5 us (9%)
  between operations  13.5 us (8%)
  starting transfers between devices  8.62 us (5%)
    all_gather x1, waiting for transfers between devices, per_device(): slab_rows = lax.all_gather(half_local, 'aux', axis=0, tiled=True)  63.7 us
    all_gather x1, waiting for transfers between devices, per_device(): all_rows = lax.all_gather(half_local, 'row', axis=1, tiled=True)  52 us
    unnamed x6, local copies, waits for them, and re-layouts  9.16 us
    dot_general x1, matrix products, per_device(): jnp.einsum('pbmsn,bsni->pbmi', tiles_five, masked, preferred_element_type...  8.17 us
    dot_general x1, matrix products, per_device(): jnp.einsum('pmi,pli->ml', slab_rows, partner, preferred_element_type=jnp....  7.35 us
    gather x1, local copies, waits for them, and re-layouts, per_device(): picked = jnp.take(coeff_blocks, local_index, axis=0)  6.55 us
    all_to_all x1, starting transfers between devices, per_device(): lax.all_to_all(split_rows, 'aux', split_axis=2, concat_axis=0, tiled=True)  4.91 us
    reshape x1, local copies, waits for them, and re-layouts, per_device(): all_rows.reshape(p_local, row_count, aux_count, share, orbitals)  4.64 us
  transfers between devices with their start and end apart: 5, of which 2 were waited for; matrix products, arithmetic and copies ran while one was open for 6% of the time, Pallas kernels for 0%

commit v1 on v0

v1 whole, which is shorter than its diff:
```python
import functools

import jax
import jax.numpy as jnp
from jax import lax
from jax.experimental import pallas as pl
from jax.experimental.pallas import tpu as pltpu
from jax.sharding import PartitionSpec as P

MESH = pl.DeviceIdType.MESH
VMEM_LIMIT = 48 * 1024 * 1024


def with_halo(block, axis):
    count = lax.axis_size(axis)
    forward = [(i, i + 1) for i in range(count - 1)]
    backward = [(target, source) for source, target in forward]
    low = lax.ppermute(block, axis, forward)
    high = lax.ppermute(block, axis, backward)
    return jnp.concatenate([low, block, high], axis=0)


def half_kernel(slots, size, index_ref, mask_ref, tiles_ref, coeff_ref, half_ref, picked):
    block = pl.program_id(0)
    for slot in range(slots):
        rows = pl.ds(slot * size, size)

        @pl.when(mask_ref[block, slot] != 0)
        def _():
            start = pl.multiple_of(index_ref[block, slot] * size, size)
            picked[rows, :] = coeff_ref[pl.ds(start, size), :]

        @pl.when(mask_ref[block, slot] == 0)
        def _():
            picked[rows, :] = jnp.zeros((size, picked.shape[1]), picked.dtype)

    half_ref[...] = jnp.dot(
        tiles_ref[...], picked[...], preferred_element_type=jnp.float32
    ).astype(half_ref.dtype)


def half_transform(tiles, coeff, index, mask):
    rows, stored = tiles.shape
    blocks, slots = index.shape
    size, orbitals = rows // blocks, coeff.shape[1]
    return pl.pallas_call(
        functools.partial(half_kernel, slots, size),
        out_shape=jax.ShapeDtypeStruct((rows, orbitals), jnp.bfloat16),
        grid_spec=pltpu.PrefetchScalarGridSpec(
            num_scalar_prefetch=2,
            grid=(blocks,),
            in_specs=[
                pl.BlockSpec((size, stored), lambda b, *_: (b, 0)),
                pl.BlockSpec(coeff.shape, lambda b, *_: (0, 0)),
            ],
            out_specs=pl.BlockSpec((size, orbitals), lambda b, *_: (b, 0)),
            scratch_shapes=[pltpu.VMEM((stored, orbitals), jnp.bfloat16)],
        ),
        compiler_params=pltpu.CompilerParams(vmem_limit_bytes=VMEM_LIMIT),
        cost_estimate=pl.CostEstimate(
            flops=2 * rows * stored * orbitals,
            bytes_accessed=2 * rows * stored + 8 * rows * orbitals,
            transcendentals=0,
        ),
    )(index, mask, tiles, coeff)


def exchange_kernel(
    n_aux, n_pos, half_ref, out_ref, slab, part, obuf,
    aux_send, aux_recv, row_send, row_recv, out_sem,
):
    a, r = lax.axis_index("aux"), lax.axis_index("row")
    core, pos = r % 2, r // 2
    sibling = r + 1 - 2 * core
    share = half_ref.shape[1]
    has_up, has_down = pos < n_pos - 1, pos > 0

    barrier = pltpu.get_barrier_semaphore()

    def greet(device):
        pl.semaphore_signal(barrier, inc=1, device_id=device, device_id_type=MESH)

    for j in range(1, n_aux):
        greet(((a + j) % n_aux, r))
    greet((a, sibling))
    pl.when(has_up)(lambda: greet((a, r + 2)))
    pl.when(has_down)(lambda: greet((a, r - 2)))
    ups, downs = (2 * n_pos - 2 - pos) // n_pos, (pos + n_pos - 1) // n_pos
    pl.semaphore_wait(barrier, n_aux + ups + downs)

    def aux_copy(k, j):
        target = (a + j) % n_aux
        quarter = (target + k) % n_aux
        return pltpu.make_async_remote_copy(
            src_ref=half_ref.at[quarter],
            dst_ref=slab.at[j - 1, quarter],
            send_sem=aux_send.at[k, j - 1],
            recv_sem=aux_recv.at[k, j - 1],
            device_id=(target, r),
            device_id_type=MESH,
        )

    def aux_arrival(k, j):
        quarter = (a + k) % n_aux
        return pltpu.make_async_remote_copy(
            src_ref=half_ref.at[quarter],
            dst_ref=slab.at[j - 1, quarter],
            send_sem=aux_send.at[k, j - 1],
            recv_sem=aux_recv.at[k, j - 1],
            device_id=((a + j) % n_aux, r),
            device_id_type=MESH,
        )

    def row_copy(way, origin, j, own=False):
        row = 2 * origin + core
        if not own:
            src = part.at[row, j]
        elif j == 0:
            src = half_ref.at[a]
        else:
            src = slab.at[j - 1, a]
        target = (r + 2, r - 2, sibling)[way]
        return pltpu.make_async_remote_copy(
            src_ref=src,
            dst_ref=part.at[row, j],
            send_sem=row_send.at[way, origin, j],
            recv_sem=row_recv.at[row, j],
            device_id=(a, target),
            device_id_type=MESH,
        )

    def arrival(row, j):
        return pltpu.make_async_remote_copy(
            src_ref=part.at[row, j],
            dst_ref=part.at[row, j],
            send_sem=row_send.at[2, row // 2, j],
            recv_sem=row_recv.at[row, j],
            device_id=(a, sibling),
            device_id_type=MESH,
        )

    def send_own(j):
        pl.when(has_up)(lambda: row_copy(0, pos, j, True).start())
        pl.when(has_down)(lambda: row_copy(1, pos, j, True).start())
        row_copy(2, pos, j, True).start()

    def relay(d, j):
        @pl.when(pos - d >= 0)
        def _():
            origin = pos - d
            arrival(2 * origin + core, j).wait_recv()
            pl.when(has_up)(lambda: row_copy(0, origin, j).start())
            row_copy(2, origin, j).start()

        @pl.when(pos + d < n_pos)
        def _():
            origin = pos + d
            arrival(2 * origin + core, j).wait_recv()
            pl.when(has_down)(lambda: row_copy(1, origin, j).start())
            row_copy(2, origin, j).start()

    def out_copy(row):
        columns = pl.ds(pl.multiple_of(row * share, share), share)
        return pltpu.make_async_copy(obuf.at[row], out_ref.at[:, columns], out_sem.at[row])

    def multiply(row, parts):
        for m in range(n_aux):
            total = None
            for j in range(n_aux):
                left = half_ref[m] if j == 0 else slab[j - 1, m]
                term = lax.dot_general(
                    left, parts(j), (((1,), (1,)), ((), ())),
                    preferred_element_type=jnp.float32,
                )
                total = term if total is None else total + term
            obuf[row, pl.ds(m * share, share), :] = total.astype(obuf.dtype)
        out_copy(row).start()

    def multiply_same(origin):
        row = 2 * origin + core
        multiply(row, lambda j: part[row, j])

    def multiply_other(origin):
        row = 2 * origin + 1 - core
        for j in range(n_aux):
            arrival(row, j).wait_recv()
        multiply(row, lambda j: part[row, j])

    def work(d, which):
        origin = pos - d if which < 2 else pos + d
        live = (origin >= 0) & (origin < n_pos)
        run = multiply_same if which % 2 == 0 else multiply_other
        pl.when(live)(lambda: run(origin))

    for j in range(1, n_aux):
        aux_copy(0, j).start()
    send_own(0)
    for j in range(1, n_aux):
        aux_arrival(0, j).wait_recv()
        send_own(j)
    for k in range(1, n_aux):
        for j in range(1, n_aux):
            aux_copy(k, j).start()
    for j in range(n_aux):
        relay(1, j)
    for k in range(1, n_aux):
        for j in range(1, n_aux):
            aux_arrival(k, j).wait_recv()
    multiply(r, lambda j: half_ref[a] if j == 0 else slab[j - 1, a])
    multiply_other(pos)

    def step(d, carry):
        for j in range(n_aux):
            relay(d, j)
            work(d - 1, j)
        return carry

    lax.fori_loop(2, n_pos, step, 0)
    for which in range(4):
        work(n_pos - 1, which)

    for k in range(n_aux):
        for j in range(1, n_aux):
            aux_copy(k, j).wait_send()
    for j in range(n_aux):
        pl.when(has_up)(lambda: row_copy(0, pos, j, True).wait_send())
        pl.when(has_down)(lambda: row_copy(1, pos, j, True).wait_send())
        row_copy(2, pos, j, True).wait_send()

    def drain(d, carry):
        for j in range(n_aux):
            @pl.when(pos - d >= 0)
            def _():
                pl.when(has_up)(lambda: row_copy(0, pos - d, j).wait_send())
                row_copy(2, pos - d, j).wait_send()

            @pl.when(pos + d < n_pos)
            def _():
                pl.when(has_down)(lambda: row_copy(1, pos + d, j).wait_send())
                row_copy(2, pos + d, j).wait_send()
        return carry

    lax.fori_loop(1, n_pos, drain, 0)

    def finish(row, carry):
        out_copy(row).wait()
        return carry

    lax.fori_loop(0, 2 * n_pos, finish, 0)


def exchange(half, n_aux, n_row):
    rows, orbitals = half.shape
    share, n_pos = rows // n_aux, n_row // 2
    return pl.pallas_call(
        functools.partial(exchange_kernel, n_aux, n_pos),
        out_shape=jax.ShapeDtypeStruct((rows, n_row * share), jnp.bfloat16),
        in_specs=[pl.BlockSpec(memory_space=pltpu.VMEM)],
        out_specs=pl.BlockSpec(memory_space=pl.ANY),
        scratch_shapes=[
            pltpu.VMEM((n_aux - 1, n_aux, share, orbitals), jnp.bfloat16),
            pltpu.VMEM((n_row, n_aux, share, orbitals), jnp.bfloat16),
            pltpu.VMEM((n_row, rows, share), jnp.bfloat16),
            pltpu.SemaphoreType.DMA((n_aux, n_aux - 1)),
            pltpu.SemaphoreType.DMA((n_aux, n_aux - 1)),
            pltpu.SemaphoreType.DMA((3, n_pos, n_aux)),
            pltpu.SemaphoreType.DMA((n_row, n_aux)),
            pltpu.SemaphoreType.DMA((n_row,)),
        ],
        compiler_params=pltpu.CompilerParams(
            collective_id=0, has_side_effects=True, vmem_limit_bytes=VMEM_LIMIT
        ),
        cost_estimate=pl.CostEstimate(
            flops=2 * rows * rows * n_row * share,
            bytes_accessed=2 * rows * n_row * share,
            transcendentals=0,
        ),
    )(half.reshape(n_aux, share, orbitals))


def per_device(b_tiles, occ_coeff, tile_blocks, screen_mask):
    rows = b_tiles.shape[1]
    blocks = tile_blocks.shape[0]
    n_aux, n_row = lax.axis_size("aux"), lax.axis_size("row")
    extended = with_halo(occ_coeff, "row")
    index = tile_blocks - (lax.axis_index("row") - 1) * blocks
    half = half_transform(b_tiles[0], extended, index, screen_mask)
    result = exchange(half, n_aux, n_row)
    return result.reshape(rows, n_row, 1, rows // n_aux)


def solution(mesh):
    in_specs = (P("aux", "row", None), P("row", None), P("row", None), P("row", None))
    out_specs = P("row", None, "aux", None)
    return jax.shard_map(
        per_device, mesh=mesh, in_specs=in_specs, out_specs=out_specs, check_vma=False
    )
```

time: 176 us -> 75.8 us (0.43)
  waiting for transfers between devices: 116 us -> 4.18 us
  Pallas kernels: 0 us -> 62.2 us
  local copies, waits for them, and re-layouts: 20.4 us -> 3.48 us
  matrix products: 15.5 us -> 0 us
  between operations: 13.5 us -> 0.05 us
  starting transfers between devices: 8.62 us -> 3.8 us
    all_gather x2 -> x0, waiting for transfers between devices: 116 us -> none  [the longest x1 63.7 us: per_device(): slab_rows = lax.all_gather(half_local, 'aux', axis=0, tiled=True)]
    pallas_call x0 -> x2, Pallas kernels: none -> 62.2 us  [the longest x1 54.3 us: exchange(): pl.pallas_call(functools.partial(exchange_kernel, n_aux, n_pos), out_shap...]
    dot_general x2 -> x0, matrix products: 15.5 us -> none  [the longest x1 8.17 us: per_device(): jnp.einsum('pbmsn,bsni->pbmi', tiles_five, masked, preferred_element_type...]
    gather x1 -> x0, local copies, waits for them, and re-layouts: 6.55 us -> none  [per_device(): picked = jnp.take(coeff_blocks, local_index, axis=0)]
    unnamed x6 -> x3, local copies, waits for them, and re-layouts: 9.16 us -> 3.48 us
    all_to_all x1 -> x0, starting transfers between devices: 4.91 us -> none  [per_device(): lax.all_to_all(split_rows, 'aux', split_axis=2, concat_axis=0, tiled=True)]
    reshape x1 -> x0, local copies, waits for them, and re-layouts: 4.64 us -> none  [per_device(): all_rows.reshape(p_local, row_count, aux_count, share, orbitals)]
    ppermute x2, waiting for transfers between devices: 0.01 us -> 4.18 us  [the longest x1 4.18 us: with_halo(): high = lax.ppermute(block, axis, backward)]
  transfers between devices with their start and end apart: 5 -> 2, of which waited for: 2 -> 1; matrix products, arithmetic and copies ran while one was open for 6% -> 1% of each run, Pallas kernels for 0% -> 0%
where the time goes in v1:
time: 75.8 us; the launch traced here: 75.5 us
  Pallas kernels  62.2 us (82%)
  waiting for transfers between devices  4.18 us (6%)
  starting transfers between devices  3.8 us (5%)
  local copies, waits for them, and re-layouts  3.48 us (5%)
  other arithmetic  1.83 us (2%)
    pallas_call x1, Pallas kernels, exchange(): pl.pallas_call(functools.partial(exchange_kernel, n_aux, n_pos), out_shap...  54.3 us
    pallas_call x1, Pallas kernels, half_transform(): pl.pallas_call(functools.partial(half_kernel, slots, size), out_shape=jax...  7.89 us
    ppermute x1, waiting for transfers between devices, with_halo(): high = lax.ppermute(block, axis, backward)  4.18 us
    unnamed x3, local copies, waits for them, and re-layouts  3.48 us
    ppermute x1, starting transfers between devices, with_halo(): low = lax.ppermute(block, axis, forward)  2.51 us
  transfers between devices with their start and end apart: 2, of which 1 were waited for; matrix products, arithmetic and copies ran while one was open for 1% of the time, Pallas kernels for 0%

profile of v1, /device:TPU:0, one launch (start us, length us, event | category | flops | bytes accessed | tf_op | source)
XLA Modules:
  0.0 75.5 jit_solution(8646638502666594970)
XLA Ops:
  0.0 0.0 copy-start
  0.0 2.5 %collective-permute-start = (bf16[1024,256]{1,0:T(8,128)(2,1)}, bf16[1024,256]{1,0:T(8,128)(2,1)S(1)}, u32[]{:S(2)}, u32[]{:S(2)}) collective-permute-start(bf16[1024,256]{1,0:T(8,128)(2,1)} %param.5), channel_id=1, source_target_pairs={{0,1},{1,2},{2,3},{3,4},{4,5},{5,6},{6,7},{8,9},{9,10},{10,11},{11... | collective-permute-start | bytes 1572872 | tf_op jit(solution)/shard_map/ppermute | solution.py:18
  2.5 1.3 %collective-permute-start.1 = (bf16[1024,256]{1,0:T(8,128)(2,1)}, bf16[1024,256]{1,0:T(8,128)(2,1)S(1)}, u32[]{:S(2)}, u32[]{:S(2)}) collective-permute-start(bf16[1024,256]{1,0:T(8,128)(2,1)} %param.5), channel_id=1, source_target_pairs={{1,0},{2,1},{3,2},{4,3},{5,4},{6,5},{7,6},{9,8},{10,9},{11,10},{12... | collective-permute-start | bytes 1572872 | tf_op jit(solution)/shard_map/ppermute | solution.py:19
  3.8 0.7 broadcast_subtract_fusion.index_ref
  4.5 0.0 collective-permute-done
  4.5 4.2 %collective-permute-done.1 = bf16[1024,256]{1,0:T(8,128)(2,1)S(1)} collective-permute-done((bf16[1024,256]{1,0:T(8,128)(2,1)}, bf16[1024,256]{1,0:T(8,128)(2,1)S(1)}, u32[]{:S(2)}, u32[]{:S(2)}) %collective-permute-start.1) | collective-permute-done | bytes 524320 | tf_op jit(solution)/shard_map/ppermute | solution.py:19
  8.7 1.1 %pad_maximum_fusion.coeff_ref = bf16[3072,256]{1,0:T(8,128)(2,1)S(1)} fusion(bf16[1024,256]{1,0:T(8,128)(2,1)S(1)} %collective-permute-done.1, bf16[1024,256]{1,0:T(8,128)(2,1)} %param.5, bf16[1024,256]{1,0:T(8,128)(2,1)S(1)} %collective-permute-done), kind=kLoop, calls=%fused_computation | loop fusion | flops 4718592 | bytes 3145728 | tf_op jit(solution)/shard_map/concatenate | solution.py:20
  9.8 0.0 copy-done
  9.9 7.9 %shard_map.46 = bf16[1024,256]{1,0:T(8,128)(2,1)S(1)} custom-call(s32[8,16]{1,0:T(8,128)S(1)} %broadcast_subtract_fusion.index_ref, s32[8,16]{1,0:T(8,128)S(1)} %copy-done, bf16[1024,2048]{1,0:T(8,128)(2,1)} %bitcast.10, bf16[3072,256]{1,0:T(8,128)(2,1)S(1)} %pad_maximum_fusion.coeff_ref), custom_call_target="tpu_custom_call" | custom-call | flops 1073741824 | bytes 6291456 | tf_op jit(solution)/shard_map/pallas_call | solution.py:46
  17.8 54.3 %shard_map.47 = bf16[1024,2048]{1,0:T(8,128)(2,1)S(1)} custom-call(bf16[4,256,256]{2,1,0:T(8,128)(2,1)S(1)} %bitcast.9), custom_call_target="tpu_custom_call" | custom-call | flops 4294967296 | bytes 4194304 | tf_op jit(solution)/shard_map/pallas_call | solution.py:255
  72.0 3.5 %copy.6 = bf16[128,8,8,256]{3,2,1,0:T(8,128)(2,1)} copy(bf16[128,8,8,256]{3,1,2,0:T(8,128)(2,1)S(1)} %bitcast.8) | data formatting | bytes 8388608
Async XLA Ops:
  0.0 9.8 %copy-start = (s32[8,16]{1,0:T(8,128)S(1)}, s32[8,16]{1,0:T(8,128)}, u32[]{:S(2)}) copy-start(s32[8,16]{1,0:T(8,128)} %mask_ref.1) | copy-start | bytes 1540
  0.0 4.5 %collective-permute-start = (bf16[1024,256]{1,0:T(8,128)(2,1)}, bf16[1024,256]{1,0:T(8,128)(2,1)S(1)}, u32[]{:S(2)}, u32[]{:S(2)}) collective-permute-start(bf16[1024,256]{1,0:T(8,128)(2,1)} %param.5), channel_id=1, source_target_pairs={{0,1},{1,2},{2,3},{3,4},{4,5},{5,6},{6,7},{8,9},{9,10},{10,11},{11... | collective-permute-start | bytes 1572872 | tf_op jit(solution)/shard_map/ppermute | solution.py:18
  2.5 6.2 %collective-permute-start.1 = (bf16[1024,256]{1,0:T(8,128)(2,1)}, bf16[1024,256]{1,0:T(8,128)(2,1)S(1)}, u32[]{:S(2)}, u32[]{:S(2)}) collective-permute-start(bf16[1024,256]{1,0:T(8,128)(2,1)} %param.5), channel_id=1, source_target_pairs={{1,0},{2,1},{3,2},{4,3},{5,4},{6,5},{7,6},{9,8},{10,9},{11,10},{12... | collective-permute-start | bytes 1572872 | tf_op jit(solution)/shard_map/ppermute | solution.py:19

commit v2 on v1

--- a/solution.py
+++ b/solution.py
@@ -201,13 +201,16 @@
     for k in range(1, n_aux):
         for j in range(1, n_aux):
             aux_copy(k, j).start()
-    for j in range(n_aux):
-        relay(1, j)
+    for d in (1, 2):
+        for j in range(n_aux):
+            relay(d, j)
     for k in range(1, n_aux):
         for j in range(1, n_aux):
             aux_arrival(k, j).wait_recv()
     multiply(r, lambda j: half_ref[a] if j == 0 else slab[j - 1, a])
     multiply_other(pos)
+    for which in range(4):
+        work(1, which)
 
     def step(d, carry):
         for j in range(n_aux):
@@ -215,7 +218,7 @@
             work(d - 1, j)
         return carry
 
-    lax.fori_loop(2, n_pos, step, 0)
+    lax.fori_loop(3, n_pos, step, 0)
     for which in range(4):
         work(n_pos - 1, which)
 

time: 75.8 us -> 72.5 us (0.956)
  Pallas kernels: 62.2 us -> 58.6 us
    pallas_call x1, Pallas kernels: 54.3 us -> 50.7 us  [exchange(): pl.pallas_call(functools.partial(exchange_kernel, n_aux, n_pos), out_shap...]
where the time goes in v2:
time: 72.5 us; the launch traced here: 71.9 us
  Pallas kernels  58.6 us (81%)
  waiting for transfers between devices  4.18 us (6%)
  starting transfers between devices  3.8 us (5%)
  local copies, waits for them, and re-layouts  3.48 us (5%)
  other arithmetic  1.83 us (3%)
    pallas_call x1, Pallas kernels, exchange(): pl.pallas_call(functools.partial(exchange_kernel, n_aux, n_pos), out_shap...  50.7 us
    pallas_call x1, Pallas kernels, half_transform(): pl.pallas_call(functools.partial(half_kernel, slots, size), out_shape=jax...  7.91 us
    ppermute x1, waiting for transfers between devices, with_halo(): high = lax.ppermute(block, axis, backward)  4.18 us
    unnamed x3, local copies, waits for them, and re-layouts  3.48 us
    ppermute x1, starting transfers between devices, with_halo(): low = lax.ppermute(block, axis, forward)  2.51 us
  transfers between devices with their start and end apart: 2, of which 1 were waited for; matrix products, arithmetic and copies ran while one was open for 1% of the time, Pallas kernels for 0%

profile of v2, /device:TPU:0, one launch (start us, length us, event | category | flops | bytes accessed | tf_op | source)
XLA Modules:
  0.0 71.9 jit_solution(14990434329804270756)
XLA Ops:
  0.0 0.0 copy-start
  0.0 2.5 %collective-permute-start = (bf16[1024,256]{1,0:T(8,128)(2,1)}, bf16[1024,256]{1,0:T(8,128)(2,1)S(1)}, u32[]{:S(2)}, u32[]{:S(2)}) collective-permute-start(bf16[1024,256]{1,0:T(8,128)(2,1)} %param.5), channel_id=1, source_target_pairs={{0,1},{1,2},{2,3},{3,4},{4,5},{5,6},{6,7},{8,9},{9,10},{10,11},{11... | collective-permute-start | bytes 1572872 | tf_op jit(solution)/shard_map/ppermute | solution.py:18
  2.5 1.3 %collective-permute-start.1 = (bf16[1024,256]{1,0:T(8,128)(2,1)}, bf16[1024,256]{1,0:T(8,128)(2,1)S(1)}, u32[]{:S(2)}, u32[]{:S(2)}) collective-permute-start(bf16[1024,256]{1,0:T(8,128)(2,1)} %param.5), channel_id=1, source_target_pairs={{1,0},{2,1},{3,2},{4,3},{5,4},{6,5},{7,6},{9,8},{10,9},{11,10},{12... | collective-permute-start | bytes 1572872 | tf_op jit(solution)/shard_map/ppermute | solution.py:19
  3.8 0.7 broadcast_subtract_fusion.index_ref
  4.5 0.0 collective-permute-done
  4.5 4.2 %collective-permute-done.1 = bf16[1024,256]{1,0:T(8,128)(2,1)S(1)} collective-permute-done((bf16[1024,256]{1,0:T(8,128)(2,1)}, bf16[1024,256]{1,0:T(8,128)(2,1)S(1)}, u32[]{:S(2)}, u32[]{:S(2)}) %collective-permute-start.1) | collective-permute-done | bytes 524320 | tf_op jit(solution)/shard_map/ppermute | solution.py:19
  8.7 1.1 %pad_maximum_fusion.coeff_ref = bf16[3072,256]{1,0:T(8,128)(2,1)S(1)} fusion(bf16[1024,256]{1,0:T(8,128)(2,1)S(1)} %collective-permute-done.1, bf16[1024,256]{1,0:T(8,128)(2,1)} %param.5, bf16[1024,256]{1,0:T(8,128)(2,1)S(1)} %collective-permute-done), kind=kLoop, calls=%fused_computation | loop fusion | flops 4718592 | bytes 3145728 | tf_op jit(solution)/shard_map/concatenate | solution.py:20
  9.8 0.0 copy-done
  9.9 7.9 %shard_map.46 = bf16[1024,256]{1,0:T(8,128)(2,1)S(1)} custom-call(s32[8,16]{1,0:T(8,128)S(1)} %broadcast_subtract_fusion.index_ref, s32[8,16]{1,0:T(8,128)S(1)} %copy-done, bf16[1024,2048]{1,0:T(8,128)(2,1)} %bitcast.10, bf16[3072,256]{1,0:T(8,128)(2,1)S(1)} %pad_maximum_fusion.coeff_ref), custom_call_target="tpu_custom_call" | custom-call | flops 1073741824 | bytes 6291456 | tf_op jit(solution)/shard_map/pallas_call | solution.py:46
  17.8 50.7 %shard_map.47 = bf16[1024,2048]{1,0:T(8,128)(2,1)S(1)} custom-call(bf16[4,256,256]{2,1,0:T(8,128)(2,1)S(1)} %bitcast.9), custom_call_target="tpu_custom_call" | custom-call | flops 4294967296 | bytes 4194304 | tf_op jit(solution)/shard_map/pallas_call | solution.py:258
  68.4 3.5 %copy.6 = bf16[128,8,8,256]{3,2,1,0:T(8,128)(2,1)} copy(bf16[128,8,8,256]{3,1,2,0:T(8,128)(2,1)S(1)} %bitcast.8) | data formatting | bytes 8388608
Async XLA Ops:
  0.0 9.8 %copy-start = (s32[8,16]{1,0:T(8,128)S(1)}, s32[8,16]{1,0:T(8,128)}, u32[]{:S(2)}) copy-start(s32[8,16]{1,0:T(8,128)} %mask_ref.1) | copy-start | bytes 1540
  0.0 4.5 %collective-permute-start = (bf16[1024,256]{1,0:T(8,128)(2,1)}, bf16[1024,256]{1,0:T(8,128)(2,1)S(1)}, u32[]{:S(2)}, u32[]{:S(2)}) collective-permute-start(bf16[1024,256]{1,0:T(8,128)(2,1)} %param.5), channel_id=1, source_target_pairs={{0,1},{1,2},{2,3},{3,4},{4,5},{5,6},{6,7},{8,9},{9,10},{10,11},{11... | collective-permute-start | bytes 1572872 | tf_op jit(solution)/shard_map/ppermute | solution.py:18
  2.5 6.2 %collective-permute-start.1 = (bf16[1024,256]{1,0:T(8,128)(2,1)}, bf16[1024,256]{1,0:T(8,128)(2,1)S(1)}, u32[]{:S(2)}, u32[]{:S(2)}) collective-permute-start(bf16[1024,256]{1,0:T(8,128)(2,1)} %param.5), channel_id=1, source_target_pairs={{1,0},{2,1},{3,2},{4,3},{5,4},{6,5},{7,6},{9,8},{10,9},{11,10},{12... | collective-permute-start | bytes 1572872 | tf_op jit(solution)/shard_map/ppermute | solution.py:19

commit v3 on v2

--- a/solution.py
+++ b/solution.py
@@ -20,23 +20,23 @@
     return jnp.concatenate([low, block, high], axis=0)
 
 
-def half_kernel(slots, size, index_ref, mask_ref, tiles_ref, coeff_ref, half_ref, picked):
+def half_kernel(slots, size, index_ref, mask_ref, tiles_ref, coeff_ref, half_ref):
     block = pl.program_id(0)
-    for slot in range(slots):
-        rows = pl.ds(slot * size, size)
-
-        @pl.when(mask_ref[block, slot] != 0)
-        def _():
-            start = pl.multiple_of(index_ref[block, slot] * size, size)
-            picked[rows, :] = coeff_ref[pl.ds(start, size), :]
-
-        @pl.when(mask_ref[block, slot] == 0)
-        def _():
-            picked[rows, :] = jnp.zeros((size, picked.shape[1]), picked.dtype)
-
-    half_ref[...] = jnp.dot(
-        tiles_ref[...], picked[...], preferred_element_type=jnp.float32
-    ).astype(half_ref.dtype)
+
+    def picked(slot):
+        start = pl.multiple_of(index_ref[block, slot] * size, size)
+        rows = coeff_ref[pl.ds(start, size), :]
+        return jnp.where(mask_ref[block, slot] != 0, rows, jnp.zeros_like(rows))
+
+    total = None
+    for slot in range(0, slots, 2):
+        pair = jnp.concatenate([picked(slot), picked(slot + 1)], axis=0)
+        term = jnp.dot(
+            tiles_ref[:, slot * size:(slot + 2) * size], pair,
+            preferred_element_type=jnp.float32,
+        )
+        total = term if total is None else total + term
+    half_ref[...] = total.astype(half_ref.dtype)
 
 
 def half_transform(tiles, coeff, index, mask):
@@ -54,7 +54,6 @@
                 pl.BlockSpec(coeff.shape, lambda b, *_: (0, 0)),
             ],
             out_specs=pl.BlockSpec((size, orbitals), lambda b, *_: (b, 0)),
-            scratch_shapes=[pltpu.VMEM((stored, orbitals), jnp.bfloat16)],
         ),
         compiler_params=pltpu.CompilerParams(vmem_limit_bytes=VMEM_LIMIT),
         cost_estimate=pl.CostEstimate(

time: 72.5 us -> 71.3 us (0.983)
  Pallas kernels: 58.6 us -> 57.6 us
    pallas_call x1, Pallas kernels: 7.91 us -> 6.63 us  [half_transform(): pl.pallas_call(functools.partial(half_kernel, slots, size), out_shape=jax...]
where the time goes in v3:
time: 71.3 us; the launch traced here: 70.9 us
  Pallas kernels  57.6 us (81%)
  waiting for transfers between devices  4.18 us (6%)
  starting transfers between devices  3.8 us (5%)
  local copies, waits for them, and re-layouts  3.48 us (5%)
  other arithmetic  1.83 us (3%)
    pallas_call x1, Pallas kernels, exchange(): pl.pallas_call(functools.partial(exchange_kernel, n_aux, n_pos), out_shap...  51 us
    pallas_call x1, Pallas kernels, half_transform(): pl.pallas_call(functools.partial(half_kernel, slots, size), out_shape=jax...  6.63 us
    ppermute x1, waiting for transfers between devices, with_halo(): high = lax.ppermute(block, axis, backward)  4.18 us
    unnamed x3, local copies, waits for them, and re-layouts  3.48 us
    ppermute x1, starting transfers between devices, with_halo(): low = lax.ppermute(block, axis, forward)  2.51 us
  transfers between devices with their start and end apart: 2, of which 1 were waited for; matrix products, arithmetic and copies ran while one was open for 1% of the time, Pallas kernels for 0%

profile of v3, /device:TPU:0, one launch (start us, length us, event | category | flops | bytes accessed | tf_op | source)
XLA Modules:
  0.0 70.9 jit_solution(11857087486327306121)
XLA Ops:
  0.0 0.0 copy-start
  0.0 2.5 %collective-permute-start = (bf16[1024,256]{1,0:T(8,128)(2,1)}, bf16[1024,256]{1,0:T(8,128)(2,1)S(1)}, u32[]{:S(2)}, u32[]{:S(2)}) collective-permute-start(bf16[1024,256]{1,0:T(8,128)(2,1)} %param.5), channel_id=1, source_target_pairs={{0,1},{1,2},{2,3},{3,4},{4,5},{5,6},{6,7},{8,9},{9,10},{10,11},{11... | collective-permute-start | bytes 1572872 | tf_op jit(solution)/shard_map/ppermute | solution.py:18
  2.5 1.3 %collective-permute-start.1 = (bf16[1024,256]{1,0:T(8,128)(2,1)}, bf16[1024,256]{1,0:T(8,128)(2,1)S(1)}, u32[]{:S(2)}, u32[]{:S(2)}) collective-permute-start(bf16[1024,256]{1,0:T(8,128)(2,1)} %param.5), channel_id=1, source_target_pairs={{1,0},{2,1},{3,2},{4,3},{5,4},{6,5},{7,6},{9,8},{10,9},{11,10},{12... | collective-permute-start | bytes 1572872 | tf_op jit(solution)/shard_map/ppermute | solution.py:19
  3.8 0.7 broadcast_subtract_fusion.index_ref
  4.5 0.0 collective-permute-done
  4.5 4.2 %collective-permute-done.1 = bf16[1024,256]{1,0:T(8,128)(2,1)S(1)} collective-permute-done((bf16[1024,256]{1,0:T(8,128)(2,1)}, bf16[1024,256]{1,0:T(8,128)(2,1)S(1)}, u32[]{:S(2)}, u32[]{:S(2)}) %collective-permute-start.1) | collective-permute-done | bytes 524320 | tf_op jit(solution)/shard_map/ppermute | solution.py:19
  8.7 1.1 %pad_maximum_fusion.coeff_ref = bf16[3072,256]{1,0:T(8,128)(2,1)S(1)} fusion(bf16[1024,256]{1,0:T(8,128)(2,1)S(1)} %collective-permute-done.1, bf16[1024,256]{1,0:T(8,128)(2,1)} %param.5, bf16[1024,256]{1,0:T(8,128)(2,1)S(1)} %collective-permute-done), kind=kLoop, calls=%fused_computation | loop fusion | flops 4718592 | bytes 3145728 | tf_op jit(solution)/shard_map/concatenate | solution.py:20
  9.8 0.0 copy-done
  9.9 6.6 %shard_map.46 = bf16[1024,256]{1,0:T(8,128)(2,1)S(1)} custom-call(s32[8,16]{1,0:T(8,128)S(1)} %broadcast_subtract_fusion.index_ref, s32[8,16]{1,0:T(8,128)S(1)} %copy-done, bf16[1024,2048]{1,0:T(8,128)(2,1)} %bitcast.10, bf16[3072,256]{1,0:T(8,128)(2,1)S(1)} %pad_maximum_fusion.coeff_ref), custom_call_target="tpu_custom_call" | custom-call | flops 1073741824 | bytes 6291456 | tf_op jit(solution)/shard_map/pallas_call | solution.py:46
  16.5 51.0 %shard_map.47 = bf16[1024,2048]{1,0:T(8,128)(2,1)S(1)} custom-call(bf16[4,256,256]{2,1,0:T(8,128)(2,1)S(1)} %bitcast.9), custom_call_target="tpu_custom_call" | custom-call | flops 4294967296 | bytes 4194304 | tf_op jit(solution)/shard_map/pallas_call | solution.py:257
  67.5 3.5 %copy.6 = bf16[128,8,8,256]{3,2,1,0:T(8,128)(2,1)} copy(bf16[128,8,8,256]{3,1,2,0:T(8,128)(2,1)S(1)} %bitcast.8) | data formatting | bytes 8388608
Async XLA Ops:
  0.0 9.8 %copy-start = (s32[8,16]{1,0:T(8,128)S(1)}, s32[8,16]{1,0:T(8,128)}, u32[]{:S(2)}) copy-start(s32[8,16]{1,0:T(8,128)} %mask_ref.1) | copy-start | bytes 1540
  0.0 4.5 %collective-permute-start = (bf16[1024,256]{1,0:T(8,128)(2,1)}, bf16[1024,256]{1,0:T(8,128)(2,1)S(1)}, u32[]{:S(2)}, u32[]{:S(2)}) collective-permute-start(bf16[1024,256]{1,0:T(8,128)(2,1)} %param.5), channel_id=1, source_target_pairs={{0,1},{1,2},{2,3},{3,4},{4,5},{5,6},{6,7},{8,9},{9,10},{10,11},{11... | collective-permute-start | bytes 1572872 | tf_op jit(solution)/shard_map/ppermute | solution.py:18
  2.5 6.2 %collective-permute-start.1 = (bf16[1024,256]{1,0:T(8,128)(2,1)}, bf16[1024,256]{1,0:T(8,128)(2,1)S(1)}, u32[]{:S(2)}, u32[]{:S(2)}) collective-permute-start(bf16[1024,256]{1,0:T(8,128)(2,1)} %param.5), channel_id=1, source_target_pairs={{1,0},{2,1},{3,2},{4,3},{5,4},{6,5},{7,6},{9,8},{10,9},{11,10},{12... | collective-permute-start | bytes 1572872 | tf_op jit(solution)/shard_map/ppermute | solution.py:19
